TPU v7x, 32 devices: a whole 2x2x4 slice. The times are simulated.
32 devices in a mesh: tr: 4 (over y, x), line: 8 (over z, core).
Axes of the slice: x: 2, y: 2, z: 4, core: 2. Of those that a mesh axis runs over, the one named last changes fastest.
Arguments:
- initial: float32 [32, 512, 512], P('line', 'tr'), may hold values from -96 to 96
- lateral: float32 [32], replicated, may hold values from 0.05 to 0.5
- vertical: float32 [32], replicated, may hold values from 0 to 512, as said below
Outputs:
- heat_field_final: float32 [32, 512, 512], P('line', 'tr')
Inputs may be any that keep to these rules, and one draw needn't show every extreme that they name: `vertical`: positive.
All inputs are finite; a program needn't handle non-finite values.
Results may differ from a plain program's by a relative error of at most 0.0003.
Values sent between devices are 32-bit elements; how exact they have to be, the bound alone decides.
A program may use at most 192 MiB of HBM per device.

v0:
```python
import functools
import math

import jax
import jax.numpy as jnp
import numpy as np
from jax import lax
from jax.experimental import pallas as pl
from jax.experimental.pallas import tpu as pltpu
from jax.sharding import PartitionSpec as P

NODES = 4
final_time = 1.0
AXES = ("line", "tr")


def talbot_nodes(node_count):
    radius = 2.0 * node_count / (5.0 * final_time)
    result = [(radius, 0.0, 0.5 * radius / node_count * math.exp(radius * final_time), 0.0)]
    for number in range(1, node_count):
        node_angle = number * math.pi / node_count
        cotangent = math.cos(node_angle) / math.sin(node_angle)
        shift_real = radius * node_angle * cotangent
        shift_imag = radius * node_angle
        sigma_term = node_angle + (node_angle * cotangent - 1.0) * cotangent
        magnitude = radius / node_count * math.exp(final_time * shift_real)
        exp_real = magnitude * math.cos(final_time * shift_imag)
        exp_imag = magnitude * math.sin(final_time * shift_imag)
        result.append(
            (
                shift_real,
                shift_imag,
                exp_real - exp_imag * sigma_term,
                exp_imag + exp_real * sigma_term,
            )
        )
    return result


def hartley(length):
    index = np.arange(length)
    angles = 2.0 * math.pi / length * ((index[:, None] * index[None, :]) % length)
    return np.cos(angles) + np.sin(angles)


def mode_values(length):
    return 4.0 * np.sin(math.pi / length * np.arange(length)) ** 2


def times(left, right):
    lr, li = left
    rr, ri = right
    if li is None and ri is None:
        return (lr * rr, None)
    if li is None:
        return (lr * rr, lr * ri)
    if ri is None:
        return (lr * rr, li * rr)
    return (lr * rr - li * ri, lr * ri + li * rr)


def plus(left, right):
    lr, li = left
    rr, ri = right
    if li is None:
        return (lr + rr, ri)
    if ri is None:
        return (lr + rr, li)
    return (lr + rr, li + ri)


def scaled(factor, value):
    return (factor * value[0], None if value[1] is None else factor * value[1])


def inverse(value):
    real, imag = value
    if imag is None:
        return (1.0 / real, None)
    norm = 1.0 / (real * real + imag * imag)
    return (real * norm, -imag * norm)


def slots(node):
    return (0, None) if node == 0 else (2 * node - 1, 2 * node)


def load(ref, node, z):
    real, imag = slots(node)
    return (ref[real, z], None if imag is None else ref[imag, z])


def store(ref, node, z, value):
    real, imag = slots(node)
    ref[real, z] = value[0]
    if imag is not None:
        ref[imag, z] = value[1]


PLANES = 2 * NODES - 1


def factor(lam, lat, vert, inv_ref, resp_ref):
    layers = resp_ref.shape[1]
    last = layers - 1
    nodes = talbot_nodes(NODES)
    shifts = [(n[0], None if k == 0 else n[1]) for k, n in enumerate(nodes)]

    def diagonal(z, below):
        base = lat[z] * lam + (below + vert[z])
        return [(base + s[0], None if s[1] is None else s[1] + jnp.zeros_like(lam)) for s in shifts]

    below = vert[last]
    carry = []
    for k, d in enumerate(diagonal(0, below)):
        inv = inverse(d)
        g = (below + jnp.zeros_like(lam), None)
        if k:
            g = (g[0], jnp.zeros_like(lam))
        store(inv_ref, k, 0, inv)
        store(resp_ref, k, 0, g)
        carry.append((inv, times(inv, g)))

    def flat(items):
        return tuple(jax.tree.leaves(items))

    tree = jax.tree.structure(carry)

    def forward(z, leaves):
        items = jax.tree.unflatten(tree, leaves)
        below = vert[z - 1]
        fresh = []
        for k, d in enumerate(diagonal(z, below)):
            inv, resp = items[k]
            inv = inverse(plus(d, scaled(-(below * below), inv)))
            g = scaled(below, resp)
            store(inv_ref, k, z, inv)
            store(resp_ref, k, z, g)
            fresh.append((inv, times(inv, g)))
        return flat(fresh)

    lax.fori_loop(1, last, forward, flat(carry))
    ones = jnp.ones_like(lam)
    start = [(ones, None if k == 0 else jnp.zeros_like(lam)) for k in range(NODES)]
    tree_up = jax.tree.structure(start)

    def upward(step, leaves):
        items = jax.tree.unflatten(tree_up, leaves)
        z = last - 1 - step
        above = vert[z]
        fresh = []
        for k in range(NODES):
            g = plus(load(resp_ref, k, z), scaled(above, items[k]))
            value = times(load(inv_ref, k, z), g)
            store(resp_ref, k, z, value)
            fresh.append(value)
        return flat(fresh)

    lax.fori_loop(0, last, upward, flat(start))
    for k, d in enumerate(diagonal(last, vert[last - 1])):
        d = plus(d, scaled(-vert[last - 1], load(resp_ref, k, last - 1)))
        d = plus(d, scaled(-vert[last], load(resp_ref, k, 0)))
        store(resp_ref, k, last, inverse(d))


def solve(src, dst, scale, vert, inv_ref, resp_ref, half_ref):
    layers = resp_ref.shape[1]
    last = layers - 1
    nodes = talbot_nodes(NODES)
    weights = [(n[2] * scale, n[3] * scale) for n in nodes]
    zero = jnp.zeros(src.shape[1:], jnp.float32)
    start = [(zero, None if k == 0 else zero) for k in range(NODES)]
    tree = jax.tree.structure(start)

    def flat(items):
        return tuple(jax.tree.leaves(items))

    def gather(z, leaves):
        items = jax.tree.unflatten(tree, leaves)
        value = (src[z], None)
        return flat([plus(items[k], times(load(resp_ref, k, z), value)) for k in range(NODES)])

    sums = jax.tree.unflatten(tree, lax.fori_loop(0, last, gather, flat(start)))
    rhs = src[last]
    roots = [times(load(resp_ref, k, last), plus(sums[k], (rhs, None))) for k in range(NODES)]

    def real_total(items):
        total = weights[0][0] * items[0][0]
        for k in range(1, NODES):
            total = total + weights[k][0] * items[k][0] - weights[k][1] * items[k][1]
        return total

    dst[last] = real_total(roots)

    def forward(z, leaves):
        items = jax.tree.unflatten(tree, leaves)
        below = vert[lax.select(z == 0, last, z - 1)]
        value = (src[z], None)
        fresh = []
        for k in range(NODES):
            g = plus(scaled(below, items[k]), value)
            store(half_ref, k, z, g)
            fresh.append(times(load(inv_ref, k, z), g))
        return flat(fresh)

    lax.fori_loop(0, last, forward, flat(roots))

    def downward(step, leaves):
        items = jax.tree.unflatten(tree, leaves)
        z = last - 1 - step
        above = vert[z]
        fresh = []
        for k in range(NODES):
            g = plus(load(half_ref, k, z), scaled(above, items[k]))
            fresh.append(times(load(inv_ref, k, z), g))
        dst[z] = real_total(fresh)
        return flat(fresh)

    lax.fori_loop(0, last, downward, flat(roots))


def solve_kernel(scale, src, lam, lat, vert, dst, inv_ref, resp_ref, half_ref):
    factor(lam[...], lat, vert, inv_ref, resp_ref)
    solve(src, dst, scale, vert, inv_ref, resp_ref, half_ref)


def vertical_solves(source, lam, lateral, vertical, scale):
    layers, rows, width = source.shape
    plane = (PLANES, layers, rows, width)
    return pl.pallas_call(
        functools.partial(solve_kernel, scale),
        out_shape=jax.ShapeDtypeStruct(source.shape, jnp.float32),
        in_specs=[pl.BlockSpec(memory_space=pltpu.VMEM)] * 2
        + [pl.BlockSpec(memory_space=pltpu.SMEM)] * 2,
        out_specs=pl.BlockSpec(memory_space=pltpu.VMEM),
        scratch_shapes=[pltpu.VMEM(plane, jnp.float32)] * 3,
        compiler_params=pltpu.CompilerParams(vmem_limit_bytes=50 * 1024 * 1024),
    )(source, lam, lateral, vertical)


def plain_path(initial, lateral, vertical):
    z_cells, x_local, y_width = initial.shape
    tr_count, line_count = lax.axis_size("tr"), lax.axis_size("line")
    peers = tr_count * line_count
    x_width = x_local * tr_count
    layers = z_cells * line_count
    y_local = y_width // peers
    high = lax.Precision.HIGH
    along_y = jnp.asarray(hartley(y_width), jnp.float32)
    along_x = jnp.asarray(hartley(x_width), jnp.float32)
    me = lax.axis_index(AXES)
    modes = jnp.einsum("zxy,qy->zqx", initial, along_y, precision=high)
    modes = modes.reshape(z_cells, peers, y_local, x_local).transpose(1, 0, 2, 3)
    modes = lax.all_to_all(modes, AXES, split_axis=0, concat_axis=0, tiled=True)
    modes = modes.reshape(line_count, tr_count, z_cells, y_local, x_local)
    modes = modes.transpose(0, 2, 3, 1, 4).reshape(layers, y_local, x_width)
    modes = jnp.einsum("zqx,xp->zqp", modes, along_x, precision=high)
    lam_y = lax.dynamic_slice_in_dim(
        jnp.asarray(mode_values(y_width), jnp.float32), me * y_local, y_local
    )
    lam = lam_y[:, None] + jnp.asarray(mode_values(x_width), jnp.float32)[None, :]
    total = vertical_solves(modes, lam, lateral, vertical, 1.0 / (x_width * y_width))
    back = jnp.einsum("zqp,px->zqx", total, along_x, precision=high)
    back = back.reshape(line_count, z_cells, y_local, tr_count, x_local)
    back = back.transpose(0, 3, 1, 2, 4).reshape(peers, z_cells, y_local, x_local)
    back = lax.all_to_all(back, AXES, split_axis=0, concat_axis=0, tiled=True)
    back = back.transpose(1, 0, 2, 3).reshape(z_cells, y_width, x_local)
    return jnp.einsum("zqx,qy->zxy", back, along_y, precision=high)


def solution(mesh):
    in_specs = (P("line", "tr", None), P(), P())
    out_specs = P("line", "tr", None)
    return jax.shard_map(
        plain_path, mesh=mesh, in_specs=in_specs, out_specs=out_specs, check_vma=False
    )
```

profile of v0, /device:TPU:0, one launch (start us, length us, event | category | flops | bytes accessed | tf_op | source)
XLA Modules:
  0.0 89.0 jit_solution(15196423595371823749)
XLA Ops:
  0.0 0.0 copy-start
  0.0 1.2 %copy-done = f32[4,128,512]{2,1,0:T(8,128)S(1)} copy-done((f32[4,128,512]{2,1,0:T(8,128)S(1)}, f32[4,128,512]{2,1,0:T(8,128)}, u32[]{:S(2)}) %copy-start) | copy-done | bytes 1048600
  1.2 2.3 %fusion = f32[512,4,128]{2,0,1:T(8,128)S(1)} fusion(f32[512,512,1]{1,0,2:T(8,128)} %constant.23, f32[4,128,512]{2,1,0:T(8,128)S(1)} %copy-done), kind=kOutput, calls=%fused_computation.2 | convolution fusion | flops 805306368 | bytes 3145728 | tf_op jit(solution)/shard_map/zxy,qy->zqx/dot_general | solution.py:252
  3.5 1.1 %copy.18 = f32[4,32,16,128]{3,2,0,1:T(8,128)} copy(f32[4,32,16,128]{3,2,1,0:T(8,128)S(1)} %bitcast.24) | data formatting | bytes 2097152 | tf_op jit(solution)/shard_map/reshape | solution.py:253
  4.6 7.3 %all-to-all-start = ((f32[32,4,16,128]{3,2,1,0:T(8,128)}), f32[32,4,16,128]{3,2,1,0:T(8,128)S(1)}, u32[]{:S(2)}, u32[]{:S(2)}) async-start(f32[32,4,16,128]{3,2,1,0:T(8,128)} %bitcast.22), calls=%async_computation | async-start | bytes 2097152 | tf_op jit(solution)/shard_map/all_to_all | solution.py:254
  11.9 0.0 copy-start.4
  11.9 0.7 copy-done.4
  12.6 0.1 dynamic_slice.3
  12.7 0.1 broadcast_add_fusion.lam
  12.7 25.6 %all-to-all-done = f32[32,4,16,128]{3,2,1,0:T(8,128)S(1)} async-done(((f32[32,4,16,128]{3,2,1,0:T(8,128)}), f32[32,4,16,128]{3,2,1,0:T(8,128)S(1)}, u32[]{:S(2)}, u32[]{:S(2)}) %all-to-all-start) | async-done | bytes 1048608 | tf_op jit(solution)/shard_map/all_to_all | solution.py:254
  38.3 1.7 %copy.12 = f32[8,4,16,4,128]{4,3,2,1,0:T(4,128)} copy(f32[8,4,16,4,128]{4,2,1,3,0:T(8,128)S(1)} %bitcast.25) | data formatting | bytes 2097152 | tf_op jit(solution)/shard_map/transpose | solution.py:256
  40.0 0.0 copy-start.3
  40.0 1.7 %reshape.22 = f32[32,16,512]{2,1,0:T(8,128)S(1)} reshape(f32[8,4,16,4,128]{4,3,2,1,0:T(4,128)} %copy.12) | data formatting | bytes 2097152 | tf_op jit(solution)/shard_map/reshape | solution.py:256
  41.7 0.0 copy-done.3
  41.7 0.0 copy-start.1
  41.8 0.0 copy-start.2
  41.8 1.0 %fusion.1.src = f32[32,16,512]{2,1,0:T(8,128)S(1)} fusion(f32[32,16,512]{2,1,0:T(8,128)S(1)} %reshape.22, f32[512,512,1]{1,0,2:T(8,128)S(1)} %copy-done.3), kind=kOutput, calls=%fused_computation.3 | convolution fusion | flops 805306368 | bytes 3145728 | tf_op jit(solution)/shard_map/zqx,xp->zqp/dot_general | solution.py:257
  42.8 0.0 copy-done.1
  42.8 0.0 copy-done.2
  42.8 10.8 %shard_map.73 = f32[32,16,512]{2,1,0:T(8,128)S(1)} custom-call(f32[32,16,512]{2,1,0:T(8,128)S(1)} %fusion.1.src, f32[16,512]{1,0:T(8,128)S(1)} %broadcast_add_fusion.lam, f32[32]{0:T(128)S(1)} %copy-done.1, f32[32]{0:T(128)S(1)} %copy-done.2), custom_call_target="tpu_custom_call" | custom-call | tf_op jit(solution)/shard_map/pallas_call | solution.py:230
  53.6 1.0 %fusion.2 = f32[32,16,512]{2,1,0:T(8,128)S(1)} fusion(f32[32,16,512]{2,1,0:T(8,128)S(1)} %shard_map.73, f32[512,512,1]{1,0,2:T(8,128)S(1)} %copy-done.3), kind=kOutput, calls=%fused_computation.4 | convolution fusion | flops 805306368 | bytes 3145728 | tf_op jit(solution)/shard_map/zqp,px->zqx/dot_general | solution.py:263
  54.6 1.3 %reshape.23 = f32[8,4,16,4,128]{4,3,2,1,0:T(4,128)} reshape(f32[32,16,512]{2,1,0:T(8,128)S(1)} %fusion.2) | data formatting | bytes 2097152 | tf_op jit(solution)/shard_map/reshape | solution.py:264
  55.9 1.3 %copy.13 = f32[8,4,16,4,128]{4,2,1,3,0:T(8,128)S(1)} copy(f32[8,4,16,4,128]{4,3,2,1,0:T(4,128)} %reshape.23) | data formatting | bytes 2097152 | tf_op jit(solution)/shard_map/reshape | solution.py:264
  57.2 29.7 %all_to_all.10 = f32[32,4,16,128]{3,2,1,0:T(8,128)S(1)} all-to-all(f32[32,4,16,128]{3,2,1,0:T(8,128)S(1)} %bitcast.26), channel_id=1, replica_groups=mesh['tr'=4,'line'=8] {'line','tr'}, dimensions={0} | all-to-all | bytes 2097152 | tf_op jit(solution)/shard_map/all_to_all | solution.py:266
  86.9 0.1 copy.14
  87.0 2.0 %fusion.3 = f32[4,128,512]{2,1,0:T(8,128)} fusion(f32[4,512,128]{2,1,0:T(8,128)S(1)} %bitcast.23, f32[512,512,1]{1,0,2:T(8,128)S(1)} %copy-done.3), kind=kOutput, calls=%fused_computation.5 | convolution fusion | flops 805306368 | bytes 3145728 | tf_op jit(solution)/shard_map/zqx,qy->zxy/dot_general | solution.py:268
Async XLA Ops:
  0.0 1.2 %copy-start = (f32[4,128,512]{2,1,0:T(8,128)S(1)}, f32[4,128,512]{2,1,0:T(8,128)}, u32[]{:S(2)}) copy-start(f32[4,128,512]{2,1,0:T(8,128)} %param.7) | copy-start | bytes 3145732
  4.6 33.7 %all-to-all-start = ((f32[32,4,16,128]{3,2,1,0:T(8,128)}), f32[32,4,16,128]{3,2,1,0:T(8,128)S(1)}, u32[]{:S(2)}, u32[]{:S(2)}) async-start(f32[32,4,16,128]{3,2,1,0:T(8,128)} %bitcast.22), calls=%async_computation | async-start | bytes 2097152 | tf_op jit(solution)/shard_map/all_to_all | solution.py:254
  11.9 0.7 copy-start.4
  40.0 1.7 %copy-start.3 = (f32[512,512,1]{1,0,2:T(8,128)S(1)}, f32[512,512,1]{1,0,2:T(8,128)}, u32[]{:S(2)}) copy-start(f32[512,512,1]{1,0,2:T(8,128)} %constant.23) | copy-start | bytes 3145732
  41.7 1.0 %copy-start.1 = (f32[32]{0:T(128)S(1)}, f32[32]{0:T(128)}, u32[]{:S(2)}) copy-start(f32[32]{0:T(128)} %lat.1) | copy-start | bytes 388
  41.8 1.0 %copy-start.2 = (f32[32]{0:T(128)S(1)}, f32[32]{0:T(128)}, u32[]{:S(2)}) copy-start(f32[32]{0:T(128)} %vert.1) | copy-start | bytes 388
where the time goes:
time: 89.4 us; the launch traced here: 89 us
  blocking collectives  29.7 us (33%)
  waiting for transfers between devices  25.6 us (29%)
  Pallas kernels  10.8 us (12%)
  local copies, waits for them, and re-layouts  9.24 us (10%)
  starting transfers between devices  7.3 us (8%)
  matrix products  6.27 us (7%)
    all_to_all x1, blocking collectives, plain_path(): back = lax.all_to_all(back, AXES, split_axis=0, concat_axis=0, tiled=True)  29.7 us
    all_to_all x1, waiting for transfers between devices, plain_path(): modes = lax.all_to_all(modes, AXES, split_axis=0, concat_axis=0, tiled=True)  25.6 us
    pallas_call x1, Pallas kernels, vertical_solves(): pl.pallas_call(functools.partial(solve_kernel, scale), out_shape=jax.Shap...  10.8 us
    all_to_all x1, starting transfers between devices, plain_path(): modes = lax.all_to_all(modes, AXES, split_axis=0, concat_axis=0, tiled=True)  7.3 us
    reshape x2, local copies, waits for them, and re-layouts, plain_path(): back = back.reshape(line_count, z_cells, y_local, tr_count, x_local)  2.65 us
    dot_general x1, matrix products, plain_path(): modes = jnp.einsum('zxy,qy->zqx', initial, along_y, precision=high)  2.25 us
    dot_general x1, matrix products, plain_path(): return jnp.einsum('zqx,qy->zxy', back, along_y, precision=high)  2 us
    unnamed x10, local copies, waits for them, and re-layouts  1.92 us
  transfers between devices with their start and end apart: 1, of which 1 were waited for; matrix products, arithmetic and copies ran while one was open for 0% of the time, Pallas kernels for 0%

commit v1 on v0

--- a/solution.py
+++ b/solution.py
@@ -268,9 +268,226 @@
     return jnp.einsum("zqx,qy->zxy", back, along_y, precision=high)
 
 
+def split(value):
+    high = value.astype(jnp.bfloat16)
+    return high, (value - high.astype(jnp.float32)).astype(jnp.bfloat16)
+
+
+def three_pass(left, right, dims):
+    def dot(a, b):
+        return lax.dot_general(a, b, (dims, ((), ())), preferred_element_type=jnp.float32)
+
+    return dot(left[0], right[0]) + (dot(left[1], right[0]) + dot(left[0], right[1]))
+
+
+ROWS = 8
+
+
+def fused_kernel(
+    scale,
+    sizes,
+    init,
+    yh,
+    yl,
+    xh,
+    xl,
+    lam_y,
+    lam_x,
+    lat,
+    vert,
+    out,
+    sent,
+    arrived,
+    modes,
+    solved,
+    replies,
+    back,
+    inv_ref,
+    resp_ref,
+    half_ref,
+    send_sem,
+    recv_sem,
+):
+    line_count, tr_count, chunks = sizes
+    peers = line_count * tr_count
+    z_cells, x_local, y_width = init.shape
+    x_width = x_local * tr_count
+    layers = z_cells * line_count
+    band = peers * ROWS
+    line, tr = lax.axis_index("line"), lax.axis_index("tr")
+    me = line * tr_count + tr
+
+    def place(index):
+        return {"line": index // tr_count, "tr": lax.rem(index, tr_count)}
+
+    def after(j):
+        return lax.rem(me + j, peers)
+
+    def before(j):
+        return lax.rem(me + peers - j, peers)
+
+    def block(ref, h, index):
+        first = pl.multiple_of((index // tr_count) * z_cells, z_cells)
+        column = pl.multiple_of(lax.rem(index, tr_count) * x_local, x_local)
+        return ref.at[h, pl.ds(first, z_cells), :, pl.ds(column, x_local)]
+
+    def rows(ref, h, index):
+        return ref.at[h, :, pl.ds(pl.multiple_of(index * ROWS, ROWS), ROWS), :]
+
+    def forth(h, src_index, dst_index, j):
+        return pltpu.make_async_remote_copy(
+            src_ref=rows(sent, h, dst_index),
+            dst_ref=block(arrived, h, src_index),
+            send_sem=send_sem.at[0, h, j],
+            recv_sem=recv_sem.at[0, h, j],
+            device_id=place(dst_index),
+            device_id_type=pl.DeviceIdType.MESH,
+        )
+
+    def reply(h, src_index, dst_index, j):
+        return pltpu.make_async_remote_copy(
+            src_ref=block(replies, h, dst_index),
+            dst_ref=rows(back, h, src_index),
+            send_sem=send_sem.at[1, h, j],
+            recv_sem=recv_sem.at[1, h, j],
+            device_id=place(dst_index),
+            device_id_type=pl.DeviceIdType.MESH,
+        )
+
+    def start_all(make, h):
+        @pl.loop(1, peers)
+        def _(j):
+            make(h, me, after(j), j).start()
+
+    def receive_all(make, h):
+        @pl.loop(1, peers)
+        def _(j):
+            make(h, before(j), me, j).wait_recv()
+
+    def sent_all(make, h):
+        @pl.loop(1, peers)
+        def _(j):
+            make(h, me, after(j), j).wait_send()
+
+    barrier = pltpu.get_barrier_semaphore()
+
+    @pl.loop(1, peers)
+    def _(j):
+        pl.semaphore_signal(
+            barrier, inc=1, device_id=place(after(j)), device_id_type=pl.DeviceIdType.MESH
+        )
+
+    source = split(init[...].reshape(z_cells * x_local, y_width))
+    for h in range(chunks):
+        part = (yh[pl.ds(h * band, band), :], yl[pl.ds(h * band, band), :])
+        spectrum = three_pass(part, source, ((1,), (1,)))
+        for z in range(z_cells):
+            sent[h, z] = spectrum[:, z * x_local : (z + 1) * x_local]
+        if h == 0:
+            pl.semaphore_wait(barrier, peers - 1)
+        start_all(forth, h)
+    for h in range(chunks):
+        block(arrived, h, me)[...] = rows(sent, h, me)[...]
+    for h in range(chunks):
+        first = pl.multiple_of(h * band + me * ROWS, ROWS)
+        lam = lam_y[pl.ds(first, ROWS), :] + lam_x[...]
+        factor(lam, lat, vert, inv_ref.at[h], resp_ref.at[h])
+    x_pair = (xh[...], xl[...])
+    for h in range(chunks):
+        receive_all(forth, h)
+        flat = split(arrived[h].reshape(layers * ROWS, x_width))
+        modes[...] = three_pass(flat, x_pair, ((1,), (0,))).reshape(layers, ROWS, x_width)
+        solve(modes, solved, scale, vert, inv_ref.at[h], resp_ref.at[h], half_ref)
+        flat = split(solved[...].reshape(layers * ROWS, x_width))
+        replies[h] = three_pass(flat, x_pair, ((1,), (0,))).reshape(layers, ROWS, x_width)
+        start_all(reply, h)
+        rows(back, h, me)[...] = block(replies, h, me)[...]
+    for h in range(chunks):
+        receive_all(reply, h)
+        part = (yh[pl.ds(h * band, band), :], yl[pl.ds(h * band, band), :])
+        wide = jnp.concatenate([back[h, z] for z in range(z_cells)], axis=1)
+        field = three_pass(split(wide.T), part, ((1,), (0,)))
+        field = field.reshape(z_cells, x_local, y_width)
+        if h == 0:
+            out[...] = field
+        else:
+            out[...] += field
+    for h in range(chunks):
+        sent_all(forth, h)
+        sent_all(reply, h)
+
+
+def halves(matrix):
+    single = np.asarray(matrix, np.float32)
+    high = single.astype(jnp.bfloat16)
+    return high, (single - high.astype(np.float32)).astype(jnp.bfloat16)
+
+
+def fused_path(initial, lateral, vertical):
+    z_cells, x_local, y_width = initial.shape
+    tr_count, line_count = lax.axis_size("tr"), lax.axis_size("line")
+    peers = tr_count * line_count
+    x_width = x_local * tr_count
+    layers = z_cells * line_count
+    chunks = y_width // (peers * ROWS)
+    yh, yl = halves(hartley(y_width))
+    xh, xl = halves(hartley(x_width))
+    lam_y = np.asarray(mode_values(y_width), np.float32)[:, None]
+    lam_x = np.asarray(mode_values(x_width), np.float32)[None, :]
+    vmem = pl.BlockSpec(memory_space=pltpu.VMEM)
+    smem = pl.BlockSpec(memory_space=pltpu.SMEM)
+    f32 = jnp.float32
+    narrow = pltpu.VMEM((chunks, z_cells, peers * ROWS, x_local), f32)
+    whole = pltpu.VMEM((chunks, layers, ROWS, x_width), f32)
+    one = pltpu.VMEM((layers, ROWS, x_width), f32)
+    planes = pltpu.VMEM((chunks, PLANES, layers, ROWS, x_width), f32)
+    return pl.pallas_call(
+        functools.partial(
+            fused_kernel, 1.0 / (x_width * y_width), (line_count, tr_count, chunks)
+        ),
+        out_shape=jax.ShapeDtypeStruct(initial.shape, f32),
+        in_specs=[vmem] * 7 + [smem] * 2,
+        out_specs=vmem,
+        scratch_shapes=[
+            narrow,
+            whole,
+            one,
+            one,
+            whole,
+            narrow,
+            planes,
+            planes,
+            pltpu.VMEM((PLANES, layers, ROWS, x_width), f32),
+            pltpu.SemaphoreType.DMA((2, chunks, peers)),
+            pltpu.SemaphoreType.DMA((2, chunks, peers)),
+        ],
+        compiler_params=pltpu.CompilerParams(
+            collective_id=0, has_side_effects=True, vmem_limit_bytes=50 * 1024 * 1024
+        ),
+        cost_estimate=pl.CostEstimate(
+            flops=24 * z_cells * x_local * y_width * y_width,
+            bytes_accessed=12 * z_cells * x_local * y_width,
+            transcendentals=0,
+        ),
+    )(
+        initial,
+        *[jnp.asarray(a) for a in (yh, yl, xh, xl, lam_y, lam_x)],
+        lateral,
+        vertical,
+    )
+
+
+def local(initial, lateral, vertical):
+    z_cells, x_local, y_width = initial.shape
+    peers = lax.axis_size("tr") * lax.axis_size("line")
+    if x_local % 128 == 0 and y_width % (peers * ROWS) == 0:
+        return fused_path(initial, lateral, vertical)
+    return plain_path(initial, lateral, vertical)
+
+
 def solution(mesh):
     in_specs = (P("line", "tr", None), P(), P())
     out_specs = P("line", "tr", None)
     return jax.shard_map(
-        plain_path, mesh=mesh, in_specs=in_specs, out_specs=out_specs, check_vma=False
+        local, mesh=mesh, in_specs=in_specs, out_specs=out_specs, check_vma=False
     )

time: 89.4 us -> 63.1 us (0.71)
  the two profiles are of different devices: /device:TPU:0 before, /device:TPU:13 now
where the time goes in v1:
time: 63.1 us; the launch traced here: 62.7 us
  Pallas kernels  55.5 us (88%)
  local copies, waits for them, and re-layouts  7.22 us (11%)
    pallas_call x1, Pallas kernels, fused_path(): pl.pallas_call(functools.partial(fused_kernel, 1.0 / (x_width * y_width),...  55.5 us
    unnamed x15, local copies, waits for them, and re-layouts  7.22 us

profile of v1, /device:TPU:13, one launch (start us, length us, event | category | flops | bytes accessed | tf_op | source)
XLA Modules:
  0.0 62.7 jit_solution(11905199423064519710)
XLA Ops:
  0.0 0.0 copy-start.6
  0.0 0.7 %copy-done.6 = f32[1,512]{1,0:T(1,128)S(1)} copy-done((f32[1,512]{1,0:T(1,128)S(1)}, f32[1,512]{1,0:T(1,128)}, u32[]{:S(2)}) %copy-start.6) | copy-done | bytes 2072
  0.7 0.0 copy-start
  0.7 1.2 %copy-done = f32[4,128,512]{2,1,0:T(8,128)S(1)} copy-done((f32[4,128,512]{2,1,0:T(8,128)S(1)}, f32[4,128,512]{2,1,0:T(8,128)}, u32[]{:S(2)}) %copy-start) | copy-done | bytes 1048600
  1.9 0.0 copy-start.1
  1.9 0.7 %copy-done.1 = f32[32]{0:T(128)S(1)} copy-done((f32[32]{0:T(128)S(1)}, f32[32]{0:T(128)}, u32[]{:S(2)}) %copy-start.1) | copy-done | bytes 152
  2.6 0.0 copy-start.2
  2.6 0.7 %copy-done.2 = f32[32]{0:T(128)S(1)} copy-done((f32[32]{0:T(128)S(1)}, f32[32]{0:T(128)}, u32[]{:S(2)}) %copy-start.2) | copy-done | bytes 152
  3.2 0.0 copy-start.3
  3.2 1.0 %copy-done.3 = bf16[512,512]{1,0:T(8,128)(2,1)S(1)} copy-done((bf16[512,512]{1,0:T(8,128)(2,1)S(1)}, bf16[512,512]{1,0:T(8,128)(2,1)}, u32[]{:S(2)}) %copy-start.3) | copy-done | bytes 524312
  4.3 0.0 copy-start.4
  4.3 1.0 %copy-done.4 = bf16[512,512]{1,0:T(8,128)(2,1)S(1)} copy-done((bf16[512,512]{1,0:T(8,128)(2,1)S(1)}, bf16[512,512]{1,0:T(8,128)(2,1)}, u32[]{:S(2)}) %copy-start.4) | copy-done | bytes 524312
  5.3 0.0 copy-start.5
  5.3 0.9 %copy-done.5 = f32[512,1]{1,0:T(8,128)S(1)} copy-done((f32[512,1]{1,0:T(8,128)S(1)}, f32[512,1]{1,0:T(8,128)}, u32[]{:S(2)}) %copy-start.5) | copy-done | bytes 2072
  6.3 55.5 %shard_map.91 = f32[4,128,512]{2,1,0:T(8,128)S(1)} custom-call(f32[4,128,512]{2,1,0:T(8,128)S(1)} %copy-done, bf16[512,512]{1,0:T(8,128)(2,1)S(1)} %copy-done.4, bf16[512,512]{1,0:T(8,128)(2,1)S(1)} %copy-done.3, bf16[512,512]{1,0:T(8,128)(2,1)S(1)} %copy-done.4, bf16[512,512]{1,0:T(8,128)(2,1)S(1)} %copy-done.3, f32[512,1]{1,0:T(8,128)S(1)} %copy-done.5, ...), custom_call_target="tpu_custom_call" | custom-call | flops 3221225472 | bytes 3145728 | tf_op jit(solution)/shard_map/pallas_call | solution.py:444
  61.8 1.0 %copy.11 = f32[4,128,512]{2,1,0:T(8,128)} copy(f32[4,128,512]{2,1,0:T(8,128)S(1)} %shard_map.91) | data formatting | bytes 2097152
Async XLA Ops:
  0.0 0.7 %copy-start.6 = (f32[1,512]{1,0:T(1,128)S(1)}, f32[1,512]{1,0:T(1,128)}, u32[]{:S(2)}) copy-start(f32[1,512]{1,0:T(1,128)} %constant.11.clone.lam_x) | copy-start | bytes 6148
  0.7 1.2 %copy-start = (f32[4,128,512]{2,1,0:T(8,128)S(1)}, f32[4,128,512]{2,1,0:T(8,128)}, u32[]{:S(2)}) copy-start(f32[4,128,512]{2,1,0:T(8,128)} %init.1) | copy-start | bytes 3145732
  1.9 0.7 %copy-start.1 = (f32[32]{0:T(128)S(1)}, f32[32]{0:T(128)}, u32[]{:S(2)}) copy-start(f32[32]{0:T(128)} %lat.1) | copy-start | bytes 388
  2.6 0.7 %copy-start.2 = (f32[32]{0:T(128)S(1)}, f32[32]{0:T(128)}, u32[]{:S(2)}) copy-start(f32[32]{0:T(128)} %vert.1) | copy-start | bytes 388
  3.2 1.0 %copy-start.3 = (bf16[512,512]{1,0:T(8,128)(2,1)S(1)}, bf16[512,512]{1,0:T(8,128)(2,1)}, u32[]{:S(2)}) copy-start(bf16[512,512]{1,0:T(8,128)(2,1)} %constant.9.clone.yl.xl) | copy-start | bytes 1572868
  4.3 1.0 %copy-start.4 = (bf16[512,512]{1,0:T(8,128)(2,1)S(1)}, bf16[512,512]{1,0:T(8,128)(2,1)}, u32[]{:S(2)}) copy-start(bf16[512,512]{1,0:T(8,128)(2,1)} %constant.8.clone.yh.xh) | copy-start | bytes 1572868
  5.3 0.9 %copy-start.5 = (f32[512,1]{1,0:T(8,128)S(1)}, f32[512,1]{1,0:T(8,128)}, u32[]{:S(2)}) copy-start(f32[512,1]{1,0:T(8,128)} %constant.10.clone.lam_y) | copy-start | bytes 6148

commit v2 on v1

--- a/solution.py
+++ b/solution.py
@@ -286,16 +286,19 @@
 def fused_kernel(
     scale,
     sizes,
+    init_hbm,
+    y_hbm,
+    x_hbm,
+    lam_hbm,
+    lat_hbm,
+    vert_hbm,
+    out,
     init,
-    yh,
-    yl,
-    xh,
-    xl,
-    lam_y,
-    lam_x,
+    y_pair,
+    x_pair,
+    lam,
     lat,
     vert,
-    out,
     sent,
     arrived,
     modes,
@@ -305,6 +308,7 @@
     inv_ref,
     resp_ref,
     half_ref,
+    load_sem,
     send_sem,
     recv_sem,
 ):
@@ -316,15 +320,38 @@
     band = peers * ROWS
     line, tr = lax.axis_index("line"), lax.axis_index("tr")
     me = line * tr_count + tr
+    side = line_count // 2
+
+    def loading(place, source, target):
+        return pltpu.make_async_copy(source, target, load_sem.at[place])
+
+    first_loads = [loading(0, init_hbm, init), loading(1, y_hbm, y_pair)]
+    later_loads = [loading(2, lat_hbm, lat), loading(3, vert_hbm, vert)]
+    for h in range(chunks):
+        own = pl.multiple_of(h * band + me * ROWS, ROWS)
+        later_loads.append(loading(4 + h, lam_hbm.at[pl.ds(own, ROWS), :], lam.at[h]))
+    if x_hbm is y_hbm:
+        x_pair = y_pair
+    else:
+        later_loads.append(loading(4 + chunks, x_hbm, x_pair))
+    for copy in first_loads + later_loads:
+        copy.start()
 
     def place(index):
         return {"line": index // tr_count, "tr": lax.rem(index, tr_count)}
 
+    def moved(j, sign):
+        flip, rest = j // (side * tr_count), lax.rem(j, side * tr_count)
+        step, turn = rest // tr_count, lax.rem(rest, tr_count)
+        half = lax.rem(line // side + flip, 2)
+        spot = lax.rem(lax.rem(line, side) + side + sign * step, side)
+        return (half * side + spot) * tr_count + lax.rem(tr + tr_count + sign * turn, tr_count)
+
     def after(j):
-        return lax.rem(me + j, peers)
+        return moved(j, 1)
 
     def before(j):
-        return lax.rem(me + peers - j, peers)
+        return moved(j, -1)
 
     def block(ref, h, index):
         first = pl.multiple_of((index // tr_count) * z_cells, z_cells)
@@ -356,7 +383,8 @@
 
     def start_all(make, h):
         @pl.loop(1, peers)
-        def _(j):
+        def _(i):
+            j = peers - i
             make(h, me, after(j), j).start()
 
     def receive_all(make, h):
@@ -377,9 +405,11 @@
             barrier, inc=1, device_id=place(after(j)), device_id_type=pl.DeviceIdType.MESH
         )
 
+    for copy in first_loads:
+        copy.wait()
     source = split(init[...].reshape(z_cells * x_local, y_width))
     for h in range(chunks):
-        part = (yh[pl.ds(h * band, band), :], yl[pl.ds(h * band, band), :])
+        part = (y_pair[0, pl.ds(h * band, band), :], y_pair[1, pl.ds(h * band, band), :])
         spectrum = three_pass(part, source, ((1,), (1,)))
         for z in range(z_cells):
             sent[h, z] = spectrum[:, z * x_local : (z + 1) * x_local]
@@ -388,11 +418,11 @@
         start_all(forth, h)
     for h in range(chunks):
         block(arrived, h, me)[...] = rows(sent, h, me)[...]
-    for h in range(chunks):
-        first = pl.multiple_of(h * band + me * ROWS, ROWS)
-        lam = lam_y[pl.ds(first, ROWS), :] + lam_x[...]
-        factor(lam, lat, vert, inv_ref.at[h], resp_ref.at[h])
-    x_pair = (xh[...], xl[...])
+    for copy in later_loads:
+        copy.wait()
+    for h in range(chunks):
+        factor(lam[h], lat, vert, inv_ref.at[h], resp_ref.at[h])
+    x_pair = (x_pair[0], x_pair[1])
     for h in range(chunks):
         receive_all(forth, h)
         flat = split(arrived[h].reshape(layers * ROWS, x_width))
@@ -404,7 +434,7 @@
         rows(back, h, me)[...] = block(replies, h, me)[...]
     for h in range(chunks):
         receive_all(reply, h)
-        part = (yh[pl.ds(h * band, band), :], yl[pl.ds(h * band, band), :])
+        part = (y_pair[0, pl.ds(h * band, band), :], y_pair[1, pl.ds(h * band, band), :])
         wide = jnp.concatenate([back[h, z] for z in range(z_cells)], axis=1)
         field = three_pass(split(wide.T), part, ((1,), (0,)))
         field = field.reshape(z_cells, x_local, y_width)
@@ -430,25 +460,38 @@
     x_width = x_local * tr_count
     layers = z_cells * line_count
     chunks = y_width // (peers * ROWS)
-    yh, yl = halves(hartley(y_width))
-    xh, xl = halves(hartley(x_width))
-    lam_y = np.asarray(mode_values(y_width), np.float32)[:, None]
-    lam_x = np.asarray(mode_values(x_width), np.float32)[None, :]
-    vmem = pl.BlockSpec(memory_space=pltpu.VMEM)
-    smem = pl.BlockSpec(memory_space=pltpu.SMEM)
+    y_pair = np.stack(halves(hartley(y_width)))
+    matrices = [jnp.asarray(y_pair)]
+    if x_width != y_width:
+        matrices.append(jnp.asarray(np.stack(halves(hartley(x_width)))))
+    lam = mode_values(y_width)[:, None] + mode_values(x_width)[None, :]
     f32 = jnp.float32
+    scratch_x = (2, x_width, x_width) if x_width != y_width else (2, 16, 128)
     narrow = pltpu.VMEM((chunks, z_cells, peers * ROWS, x_local), f32)
     whole = pltpu.VMEM((chunks, layers, ROWS, x_width), f32)
     one = pltpu.VMEM((layers, ROWS, x_width), f32)
     planes = pltpu.VMEM((chunks, PLANES, layers, ROWS, x_width), f32)
+    body = functools.partial(
+        fused_kernel, 1.0 / (x_width * y_width), (line_count, tr_count, chunks)
+    )
+
+    def kernel(init, y_ref, *rest):
+        if len(matrices) == 1:
+            rest = (y_ref,) + rest
+        body(init, y_ref, *rest)
+
     return pl.pallas_call(
-        functools.partial(
-            fused_kernel, 1.0 / (x_width * y_width), (line_count, tr_count, chunks)
-        ),
+        kernel,
         out_shape=jax.ShapeDtypeStruct(initial.shape, f32),
-        in_specs=[vmem] * 7 + [smem] * 2,
-        out_specs=vmem,
+        in_specs=[pl.BlockSpec(memory_space=pltpu.HBM)] * (4 + len(matrices)),
+        out_specs=pl.BlockSpec(memory_space=pltpu.VMEM),
         scratch_shapes=[
+            pltpu.VMEM(initial.shape, f32),
+            pltpu.VMEM(y_pair.shape, jnp.bfloat16),
+            pltpu.VMEM(scratch_x, jnp.bfloat16),
+            pltpu.VMEM((chunks, ROWS, x_width), f32),
+            pltpu.SMEM((layers,), f32),
+            pltpu.SMEM((layers,), f32),
             narrow,
             whole,
             one,
@@ -458,11 +501,12 @@
             planes,
             planes,
             pltpu.VMEM((PLANES, layers, ROWS, x_width), f32),
+            pltpu.SemaphoreType.DMA((5 + chunks,)),
             pltpu.SemaphoreType.DMA((2, chunks, peers)),
             pltpu.SemaphoreType.DMA((2, chunks, peers)),
         ],
         compiler_params=pltpu.CompilerParams(
-            collective_id=0, has_side_effects=True, vmem_limit_bytes=50 * 1024 * 1024
+            collective_id=0, has_side_effects=True, vmem_limit_bytes=60 * 1024 * 1024
         ),
         cost_estimate=pl.CostEstimate(
             flops=24 * z_cells * x_local * y_width * y_width,
@@ -471,7 +515,8 @@
         ),
     )(
         initial,
-        *[jnp.asarray(a) for a in (yh, yl, xh, xl, lam_y, lam_x)],
+        *matrices,
+        jnp.asarray(lam, f32),
         lateral,
         vertical,
     )
@@ -480,7 +525,8 @@
 def local(initial, lateral, vertical):
     z_cells, x_local, y_width = initial.shape
     peers = lax.axis_size("tr") * lax.axis_size("line")
-    if x_local % 128 == 0 and y_width % (peers * ROWS) == 0:
+    even = lax.axis_size("line") % 2 == 0
+    if even and x_local % 128 == 0 and y_width % (peers * ROWS) == 0:
         return fused_path(initial, lateral, vertical)
     return plain_path(initial, lateral, vertical)
 

time: 63.1 us -> 61.2 us (0.970)
  the two profiles are of different devices: /device:TPU:13 before, /device:TPU:0 now
where the time goes in v2:
time: 61.2 us; the launch traced here: 61 us
  Pallas kernels  58.7 us (96%)
  local copies, waits for them, and re-layouts  2.26 us (4%)
    pallas_call x1, Pallas kernels, fused_path(): pl.pallas_call(kernel, out_shape=jax.ShapeDtypeStruct(initial.shape, f32)...  58.7 us
    unnamed x1, local copies, waits for them, and re-layouts  2.26 us

profile of v2, /device:TPU:0, one launch (start us, length us, event | category | flops | bytes accessed | tf_op | source)
XLA Modules:
  0.0 61.0 jit_solution(9044793251601622338)
XLA Ops:
  0.0 58.7 %shard_map.55 = f32[4,128,512]{2,1,0:T(8,128)} custom-call(f32[4,128,512]{2,1,0:T(8,128)} %init.1, bf16[2,512,512]{2,1,0:T(8,128)(2,1)} %constant.4.clone.y_ref, f32[512,512]{1,0:T(8,128)} %constant.5.clone.rest_0_, f32[32]{0:T(128)} %rest_1_.1, f32[32]{0:T(128)} %rest_2_.1), custom_call_target="tpu_custom_call" | custom-call | flops 3221225472 | bytes 3145728 | tf_op jit(solution)/shard_map/pallas_call | solution.py:483
  58.7 2.3 %copy.7 = f32[4,128,512]{2,1,0:T(8,128)} copy(f32[4,128,512]{2,1,0:T(8,128)} %shard_map.55) | data formatting | bytes 2097152

commit v3 on v2

--- a/solution.py
+++ b/solution.py
@@ -320,7 +320,6 @@
     band = peers * ROWS
     line, tr = lax.axis_index("line"), lax.axis_index("tr")
     me = line * tr_count + tr
-    side = line_count // 2
 
     def loading(place, source, target):
         return pltpu.make_async_copy(source, target, load_sem.at[place])
@@ -340,18 +339,11 @@
     def place(index):
         return {"line": index // tr_count, "tr": lax.rem(index, tr_count)}
 
-    def moved(j, sign):
-        flip, rest = j // (side * tr_count), lax.rem(j, side * tr_count)
-        step, turn = rest // tr_count, lax.rem(rest, tr_count)
-        half = lax.rem(line // side + flip, 2)
-        spot = lax.rem(lax.rem(line, side) + side + sign * step, side)
-        return (half * side + spot) * tr_count + lax.rem(tr + tr_count + sign * turn, tr_count)
-
     def after(j):
-        return moved(j, 1)
+        return lax.rem(me + j, peers)
 
     def before(j):
-        return moved(j, -1)
+        return lax.rem(me + peers - j, peers)
 
     def block(ref, h, index):
         first = pl.multiple_of((index // tr_count) * z_cells, z_cells)
@@ -383,8 +375,7 @@
 
     def start_all(make, h):
         @pl.loop(1, peers)
-        def _(i):
-            j = peers - i
+        def _(j):
             make(h, me, after(j), j).start()
 
     def receive_all(make, h):
@@ -506,7 +497,7 @@
             pltpu.SemaphoreType.DMA((2, chunks, peers)),
         ],
         compiler_params=pltpu.CompilerParams(
-            collective_id=0, has_side_effects=True, vmem_limit_bytes=60 * 1024 * 1024
+            collective_id=0, has_side_effects=True, vmem_limit_bytes=52 * 1024 * 1024
         ),
         cost_estimate=pl.CostEstimate(
             flops=24 * z_cells * x_local * y_width * y_width,
@@ -525,8 +516,7 @@
 def local(initial, lateral, vertical):
     z_cells, x_local, y_width = initial.shape
     peers = lax.axis_size("tr") * lax.axis_size("line")
-    even = lax.axis_size("line") % 2 == 0
-    if even and x_local % 128 == 0 and y_width % (peers * ROWS) == 0:
+    if x_local % 128 == 0 and y_width % (peers * ROWS) == 0:
         return fused_path(initial, lateral, vertical)
     return plain_path(initial, lateral, vertical)
 

time: 61.2 us -> 57.5 us (0.940)
  the two profiles are of different devices: /device:TPU:0 before, /device:TPU:13 now
where the time goes in v3:
time: 57.5 us; the launch traced here: 57.4 us
  Pallas kernels  55.1 us (96%)
  local copies, waits for them, and re-layouts  2.28 us (4%)
    pallas_call x1, Pallas kernels, fused_path(): pl.pallas_call(kernel, out_shape=jax.ShapeDtypeStruct(initial.shape, f32)...  55.1 us
    unnamed x5, local copies, waits for them, and re-layouts  2.28 us

profile of v3, /device:TPU:13, one launch (start us, length us, event | category | flops | bytes accessed | tf_op | source)
XLA Modules:
  0.0 57.4 jit_solution(1106779075844155453)
XLA Ops:
  0.0 0.0 copy-start
  0.0 0.7 %copy-done = f32[32]{0:T(128)S(1)} copy-done((f32[32]{0:T(128)S(1)}, f32[32]{0:T(128)}, u32[]{:S(2)}) %copy-start) | copy-done | bytes 152
  0.7 0.0 copy-start.1
  0.7 0.7 %copy-done.1 = f32[32]{0:T(128)S(1)} copy-done((f32[32]{0:T(128)S(1)}, f32[32]{0:T(128)}, u32[]{:S(2)}) %copy-start.1) | copy-done | bytes 152
  1.3 55.1 %shard_map.55 = f32[4,128,512]{2,1,0:T(8,128)S(1)} custom-call(f32[4,128,512]{2,1,0:T(8,128)} %init.1, bf16[2,512,512]{2,1,0:T(8,128)(2,1)} %constant.4.clone.y_ref, f32[512,512]{1,0:T(8,128)} %constant.5.clone.rest_0_, f32[32]{0:T(128)S(1)} %copy-done, f32[32]{0:T(128)S(1)} %copy-done.1), custom_call_target="tpu_custom_call" | custom-call | flops 3221225472 | bytes 3145728 | tf_op jit(solution)/shard_map/pallas_call | solution.py:474
  56.4 1.0 %copy.7 = f32[4,128,512]{2,1,0:T(8,128)} copy(f32[4,128,512]{2,1,0:T(8,128)S(1)} %shard_map.55) | data formatting | bytes 2097152
Async XLA Ops:
  0.0 0.7 %copy-start = (f32[32]{0:T(128)S(1)}, f32[32]{0:T(128)}, u32[]{:S(2)}) copy-start(f32[32]{0:T(128)} %rest_1_.1) | copy-start | bytes 388
  0.7 0.7 %copy-start.1 = (f32[32]{0:T(128)S(1)}, f32[32]{0:T(128)}, u32[]{:S(2)}) copy-start(f32[32]{0:T(128)} %rest_2_.1) | copy-start | bytes 388

commit v4 on v3

--- a/solution.py
+++ b/solution.py
@@ -290,15 +290,13 @@
     y_hbm,
     x_hbm,
     lam_hbm,
-    lat_hbm,
-    vert_hbm,
+    faces_hbm,
     out,
     init,
     y_pair,
     x_pair,
     lam,
-    lat,
-    vert,
+    faces,
     sent,
     arrived,
     modes,
@@ -325,7 +323,8 @@
         return pltpu.make_async_copy(source, target, load_sem.at[place])
 
     first_loads = [loading(0, init_hbm, init), loading(1, y_hbm, y_pair)]
-    later_loads = [loading(2, lat_hbm, lat), loading(3, vert_hbm, vert)]
+    later_loads = [loading(2, faces_hbm, faces)]
+    lat, vert = faces.at[0], faces.at[1]
     for h in range(chunks):
         own = pl.multiple_of(h * band + me * ROWS, ROWS)
         later_loads.append(loading(4 + h, lam_hbm.at[pl.ds(own, ROWS), :], lam.at[h]))
@@ -474,15 +473,14 @@
     return pl.pallas_call(
         kernel,
         out_shape=jax.ShapeDtypeStruct(initial.shape, f32),
-        in_specs=[pl.BlockSpec(memory_space=pltpu.HBM)] * (4 + len(matrices)),
+        in_specs=[pl.BlockSpec(memory_space=pltpu.HBM)] * (3 + len(matrices)),
         out_specs=pl.BlockSpec(memory_space=pltpu.VMEM),
         scratch_shapes=[
             pltpu.VMEM(initial.shape, f32),
             pltpu.VMEM(y_pair.shape, jnp.bfloat16),
             pltpu.VMEM(scratch_x, jnp.bfloat16),
             pltpu.VMEM((chunks, ROWS, x_width), f32),
-            pltpu.SMEM((layers,), f32),
-            pltpu.SMEM((layers,), f32),
+            pltpu.SMEM((2, layers), f32),
             narrow,
             whole,
             one,
@@ -508,8 +506,7 @@
         initial,
         *matrices,
         jnp.asarray(lam, f32),
-        lateral,
-        vertical,
+        jnp.stack([lateral, vertical]),
     )
 
 

time: 57.5 us -> 56.9 us (0.990)
  local copies, waits for them, and re-layouts: 2.28 us -> 1.64 us
    unnamed x5, local copies, waits for them, and re-layouts: 2.28 us -> 1.64 us
where the time goes in v4:
time: 56.9 us; the launch traced here: 56.7 us
  Pallas kernels  55 us (97%)
  local copies, waits for them, and re-layouts  1.64 us (3%)
    pallas_call x1, Pallas kernels, fused_path(): pl.pallas_call(kernel, out_shape=jax.ShapeDtypeStruct(initial.shape, f32)...  55 us
    unnamed x5, local copies, waits for them, and re-layouts  1.64 us

profile of v4, /device:TPU:13, one launch (start us, length us, event | category | flops | bytes accessed | tf_op | source)
XLA Modules:
  0.0 56.7 jit_solution(5648160000894617379)
XLA Ops:
  0.0 0.0 copy-start
  0.0 0.0 copy-start.1
  0.0 0.7 %copy-done = f32[32]{0:T(128)S(1)} copy-done((f32[32]{0:T(128)S(1)}, f32[32]{0:T(128)}, u32[]{:S(2)}) %copy-start) | copy-done | bytes 152
  0.7 0.0 copy-done.1
  0.7 55.0 %shard_map.55 = f32[4,128,512]{2,1,0:T(8,128)S(1)} custom-call(f32[4,128,512]{2,1,0:T(8,128)} %init.1, bf16[2,512,512]{2,1,0:T(8,128)(2,1)} %constant.4.clone.y_ref, f32[512,512]{1,0:T(8,128)} %constant.5.clone.rest_0_, f32[2,32]{1,0:T(2,128)S(1)} %pad_maximum_fusion.rest_1_), custom_call_target="tpu_custom_call" | custom-call | flops 3221225472 | bytes 3145728 | tf_op jit(solution)/shard_map/pallas_call | solution.py:473
  55.7 1.0 %copy.7 = f32[4,128,512]{2,1,0:T(8,128)} copy(f32[4,128,512]{2,1,0:T(8,128)S(1)} %shard_map.55) | data formatting | bytes 2097152
  (1 shorter events, 0.0 us)
Async XLA Ops:
  0.0 0.7 %copy-start = (f32[32]{0:T(128)S(1)}, f32[32]{0:T(128)}, u32[]{:S(2)}) copy-start(f32[32]{0:T(128)} %param.7) | copy-start | bytes 388
  0.0 0.7 %copy-start.1 = (f32[32]{0:T(128)S(1)}, f32[32]{0:T(128)}, u32[]{:S(2)}) copy-start(f32[32]{0:T(128)} %param.6) | copy-start | bytes 388
